TPU v7x, 256 devices: a whole 4x4x8 slice. The times are simulated.
256 devices in a mesh: wide: 32 (over x_lo, z, core), narrow: 8 (over x_hi, y).
Axes of the slice: x: 4 (x_hi: 2, x_lo: 2; x = x_hi * 2 + x_lo), y: 4, z: 8, core: 2. Of those that a mesh axis runs over, the one named last changes fastest.
Arguments:
- activations: float32 [1024, 17408], P('wide', 'narrow'), may hold values from -6 to 6
- act_basis: float32 [17408, 17408], P('narrow', 'wide'), may hold values from -0.046875 to 0.046875
- grads: float32 [1024, 5120], P(None, 'wide'), may hold values from -0.3 to 0.3
- grad_basis: float32 [5120, 5120], P('wide', 'narrow'), may hold values from -0.078125 to 0.078125
- seq_ids: int32 [1024], replicated, may hold values from 0 to 3, never falling along the last dimension, each value on 1 to 512 neighbouring positions
Outputs:
- eigenvalues: float32 [17408, 5120], P('wide', 'narrow')
Inputs may be any that keep to these rules, and one draw needn't show every extreme that they name: `seq_ids`: never falling along the rows; every sequence has at least one row and at most 512 rows, and one sequence has exactly 512.
All inputs are finite; a program needn't handle non-finite values.
Results may differ from a plain program's by a relative error of at most 0.0003.
Values sent between devices are 32-bit elements; how exact they have to be, the bound alone decides.
No kernel may reach another device: no remote copies, remote signals or barrier semaphores. Data moves between devices by JAX's collectives and lax.ppermute only.
A program may use at most 64 MiB of HBM per device.

v0:
```python
import jax
import jax.numpy as jnp
from jax import lax
from jax.sharding import Mesh
from jax.sharding import PartitionSpec as P

SEQS = 4
SEQ_MOST = 512
WIDE = ("wide_0", "wide_1", "wide_2")


def filled_up(lines, devices):
    spare = -len(lines) % devices
    return jnp.pad(lines, [(0, spare)] + [(0, 0)] * (lines.ndim - 1))


def from_everyone(value, axis):
    devices = lax.axis_size(axis)
    return lax.all_to_all(
        jnp.broadcast_to(value[None], (devices, *value.shape)), axis, 0, 0, tiled=True
    )


def in_order(blocks, dim):
    blocks = jnp.moveaxis(blocks, 0, dim)
    dims = blocks.shape
    return blocks.reshape(*dims[:dim], dims[dim] * dims[dim + 1], *dims[dim + 2 :])


def gather_axes(value, axes, dim):
    far, near = axes
    first = from_everyone(value, far)
    blocks = jnp.swapaxes(from_everyone(first, near), 0, 1)
    return in_order(blocks.reshape(-1, *value.shape), dim)


def in_blocks(value, dim, devices):
    dims = value.shape
    blocks = value.reshape(*dims[:dim], devices, dims[dim] // devices, *dims[dim + 1 :])
    return jnp.moveaxis(blocks, dim, 0)


def sent_and_summed(value, axis, dim):
    blocks = in_blocks(value, dim, lax.axis_size(axis))
    arrived = lax.all_to_all(blocks, axis, split_axis=0, concat_axis=0, tiled=True)
    return arrived.sum(axis=0)


def summed_rows(value, axes, dim):
    far, near = axes
    blocks = in_blocks(value, dim, lax.axis_size(far))
    nearer = sent_and_summed(blocks, near, dim + 1)
    arrived = lax.all_to_all(nearer, far, split_axis=0, concat_axis=0, tiled=True)
    return arrived.sum(axis=0)


def nested_sum(value, axes):
    lines = value.reshape(-1, value.shape[-1])
    padded = filled_up(lines, lax.axis_size(axes[0]) * lax.axis_size(axes[1]))
    whole = gather_axes(summed_rows(padded, axes, 0), axes, 0)
    return lax.slice_in_dim(whole, 0, len(lines)).reshape(value.shape)


def seq_window(rotated_acts, rotated_grads, seq_ids, seq_label):
    token_rows = rotated_grads.shape[0]
    first_row = jnp.sum((seq_ids < seq_label).astype(jnp.int32))
    window_start = jnp.minimum(first_row, token_rows - SEQ_MOST)
    acts_window = lax.dynamic_slice_in_dim(rotated_acts, window_start, SEQ_MOST, 0)
    grads_window = lax.dynamic_slice_in_dim(rotated_grads, window_start, SEQ_MOST, 0)
    ids_window = lax.dynamic_slice_in_dim(seq_ids, window_start, SEQ_MOST, 0)
    seq_mask = (ids_window == seq_label).astype(jnp.float32)[:, None]
    return (acts_window, grads_window * seq_mask)


def per_device(activations, act_basis, grads, grad_basis, seq_ids):
    highest = lax.Precision.HIGHEST
    gathered = lax.all_gather(activations, WIDE, axis=0, tiled=True)
    partial_acts = jnp.dot(
        gathered, act_basis, precision=highest, preferred_element_type=jnp.float32
    )
    rotated_acts = lax.psum(partial_acts, "narrow")
    partial_grads = jnp.dot(
        grads, grad_basis, precision=highest, preferred_element_type=jnp.float32
    )
    rotated_grads = nested_sum(partial_grads, (("wide_0", "wide_1"), "wide_2"))
    out_cols = rotated_grads.shape[1]
    running = jnp.zeros((rotated_acts.shape[1], out_cols), jnp.float32)
    for seq_label in range(SEQS):
        acts_window, grads_window = seq_window(rotated_acts, rotated_grads, seq_ids, seq_label)
        moment = jnp.dot(
            acts_window.T, grads_window, precision=highest, preferred_element_type=jnp.float32
        )
        running = running + moment * moment
    return running / jnp.float32(SEQS)


def solution(mesh):
    split = Mesh(
        mesh.devices.reshape(2, 8, 2, mesh.shape["narrow"]),
        ("wide_0", "wide_1", "wide_2", "narrow"),
    )
    return jax.shard_map(
        per_device,
        mesh=split,
        in_specs=(P(WIDE, "narrow"), P("narrow", WIDE), P(None, WIDE), P(WIDE, "narrow"), P()),
        out_specs=P(WIDE, "narrow"),
        check_vma=False,
    )
```

profile of v0, /device:TPU:32, one launch (start us, length us, event | category | flops | bytes accessed | tf_op | source)
XLA Modules:
  0.0 276.0 jit_solution(7294936986308628746)
XLA Ops:
  6.5 0.0 copy-start
  6.5 0.0 all-gather.2.cloned.1.call-start
  6.5 0.7 all-gather.2.cloned.1.call-update
  7.3 0.4 copy-done
  7.6 3.9 %fusion.29 = f32[1024,640]{1,0:T(8,128)S(1)} fusion(f32[1024,160]{0,1:T(8,128)S(1)} %copy-done, f32[160,640]{1,0:T(8,128)} %param.8), kind=kOutput, calls=%fused_computation.42 | convolution fusion | flops 1258291200 | bytes 3686400 | tf_op jit(solution)/shard_map/dot_general | solution.py:82
  11.6 0.2 copy.11
  11.8 5.8 %all_to_all.20 = f32[2,16,32,640]{3,2,1,0:T(8,128)S(1)} all-to-all(f32[2,16,32,640]{3,2,1,0:T(8,128)S(1)} %bitcast.15), channel_id=1, replica_groups=mesh['wide_0'=2,'wide_1'=8,'wide_2'=2,'narrow'=8] {'wide_2'}, dimensions={0} | all-to-all | bytes 5242880 | tf_op jit(solution)/shard_map/all_to_all | solution.py:45
  17.6 1.3 reduce_sum.55
  18.9 54.5 %all_to_all.21 = f32[16,32,640]{2,1,0:T(8,128)S(1)} all-to-all(f32[16,32,640]{2,1,0:T(8,128)} %reduce_sum.55), channel_id=1, replica_groups=mesh['wide_0'=2,'wide_1'=8,'wide_2'=2,'narrow'=8] {'wide_0','wide_1'}, dimensions={0} | all-to-all | bytes 2621440 | tf_op jit(solution)/shard_map/all_to_all | solution.py:53
  73.5 0.1 reduce_sum.56
  73.5 1.2 broadcast_in_dim.4
  74.7 6.4 %all-to-all-start.2 = ((f32[16,32,640]{2,1,0:T(8,128)}), f32[16,32,640]{2,1,0:T(8,128)S(1)}, u32[]{:S(2)}, u32[]{:S(2)}) async-start(f32[16,32,640]{2,1,0:T(8,128)} %broadcast_in_dim.4), calls=%async_computation.2 | async-start | bytes 2621440 | tf_op jit(solution)/shard_map/all_to_all | solution.py:19
  81.2 0.0 all-reduce.2.cloned.1.call-start
  81.2 52.6 %all-gather.2.cloned.1.call-done = f32[1024,2176]{1,0:T(8,128)} async-done(((f32[32,2176]{1,0:T(8,128)}), f32[1024,2176]{1,0:T(8,128)}) %all-gather.2.cloned.1.call-update) | async-done | bytes 8912912 | tf_op jit(solution)/shard_map/all_gather | solution.py:77
  133.8 21.9 %fusion.28 = f32[1024,544]{0,1:T(8,128)} fusion(f32[1024,2176]{1,0:T(8,128)} %all-gather.2.cloned.1.call-done, f32[2176,544]{0,1:T(8,128)} %param.6), kind=kOutput, calls=%fused_computation.41 | convolution fusion | flops 14545846272 | bytes 15876096 | tf_op jit(solution)/shard_map/dot_general | solution.py:78
  155.7 0.0 copy-start.2
  155.7 0.0 all-reduce.2.cloned.1.call-update
  155.7 0.7 copy-done.2
  156.4 0.7 convert_reduce_fusion
  159.8 0.1 fusion.27
  159.9 0.0 all-to-all-done.2
  159.9 0.3 broadcast_in_dim.5
  160.2 5.8 %all_to_all.22 = f32[2,16,32,640]{3,2,1,0:T(8,128)S(1)} all-to-all(f32[2,16,32,640]{3,2,1,0:T(8,128)S(1)} %broadcast_in_dim.5), channel_id=1, replica_groups=mesh['wide_0'=2,'wide_1'=8,'wide_2'=2,'narrow'=8] {'wide_2'}, dimensions={0} | all-to-all | bytes 5242880 | tf_op jit(solution)/shard_map/all_to_all | solution.py:19
  166.0 0.2 copy.9
  166.2 87.8 %all-reduce.2.cloned.1.call-done = f32[1024,544]{0,1:T(8,128)} async-done(((f32[1024,544]{0,1:T(8,128)}), f32[1024,544]{0,1:T(8,128)}) %all-reduce.2.cloned.1.call-update) | async-done | bytes 2228240 | tf_op jit(solution)/shard_map/psum | solution.py:81
  254.0 0.0 copy-start.1
  254.0 4.5 %convolution_multiply_fusion.1 = f32[544,640]{1,0:T(8,128)S(1)} fusion(f32[1024,640]{1,0:T(8,128)S(1)} %bitcast.11, s32[]{:T(128)S(6)} %select_n.10, f32[1024,544]{0,1:T(8,128)} %all-reduce.2.cloned.1.call-done, f32[512]{0:T(512)S(1)} %get-tuple-element.10), kind=kOutput, calls=%fused_computation.2 | convolution fusion | flops 2139770880 | bytes 3820544 | tf_op jit(solution)/shard_map/dot_general | solution.py:90
  258.5 0.0 copy-done.1
  258.5 3.1 %convolution_multiply_fusion.2 = f32[544,640]{1,0:T(8,128)S(1)} fusion(f32[1024,640]{1,0:T(8,128)S(1)} %bitcast.12, s32[]{:T(128)S(6)} %select_n.9, f32[1024,544]{0,1:T(8,128)S(1)} %copy-done.1, f32[512]{0:T(512)S(1)} %get-tuple-element.12), kind=kOutput, calls=%fused_computation.3 | convolution fusion | flops 2139770880 | bytes 3820544 | tf_op jit(solution)/shard_map/dot_general | solution.py:90
  261.7 3.2 %fusion.1 = f32[544,640]{1,0:T(8,128)S(1)} fusion(f32[544,640]{1,0:T(8,128)S(1)} %convolution_multiply_fusion.1, f32[544,640]{1,0:T(8,128)S(1)} %convolution_multiply_fusion.2, f32[1024,640]{1,0:T(8,128)S(1)} %bitcast.13, s32[]{:T(128)S(6)} %select_n.8, f32[1024,544]{0,1:T(8,128)S(1)} %copy-done.1, f32[512]{0:T(512)S(1)} %get-tuple-element.11), kind=kOutput, calls=%fused_computation.6 | convolution fusion | flops 2140467200 | bytes 6605824 | tf_op jit(solution)/shard_map/dot_general | solution.py:90
  264.9 4.2 %fusion.3 = f32[544,640]{1,0:T(8,128)} fusion(f32[544,640]{1,0:T(8,128)S(1)} %fusion.1, f32[1024,640]{1,0:T(8,128)S(1)} %bitcast.14, s32[]{:T(128)S(6)} %select_n.11, f32[1024,544]{0,1:T(8,128)S(1)} %copy-done.1, f32[512]{0:T(512)S(1)} %get-tuple-element.9), kind=kOutput, calls=%fused_computation.8 | convolution fusion | flops 2140467200 | bytes 5213184 | tf_op jit(solution)/shard_map/dot_general | solution.py:90
Async XLA Ops:
  6.5 1.1 copy-start
  6.5 127.2 %all-gather.2.cloned.1.call-start = ((), (), s32[]{:S(2)}) async-start(), calls=%async_computation.4 | async-start | bytes 9191424 | tf_op jit(solution)/shard_map/all_gather | solution.py:77
  74.7 85.1 %all-to-all-start.2 = ((f32[16,32,640]{2,1,0:T(8,128)}), f32[16,32,640]{2,1,0:T(8,128)S(1)}, u32[]{:S(2)}, u32[]{:S(2)}) async-start(f32[16,32,640]{2,1,0:T(8,128)} %broadcast_in_dim.4), calls=%async_computation.2 | async-start | bytes 2621440 | tf_op jit(solution)/shard_map/all_to_all | solution.py:19
  81.2 172.9 %all-reduce.2.cloned.1.call-start = ((), (), s32[]{:S(2)}) async-start(), calls=%async_computation.5 | async-start | bytes 4456448 | tf_op jit(solution)/shard_map/psum | solution.py:81
  155.7 0.7 copy-start.2
  254.0 4.5 %copy-start.1 = (f32[1024,544]{0,1:T(8,128)S(1)}, f32[1024,544]{0,1:T(8,128)}, u32[]{:S(2)}) copy-start(f32[1024,544]{0,1:T(8,128)} %all-reduce.2.cloned.1.call-done) | copy-start | bytes 6684676
Sparse Core Ops, SparseCore 0:
  9.2 124.5 all-gather.1
  155.9 98.0 all-reduce.1
where the time goes:
time: 276 us
  waiting for transfers between devices  141 us (51%)
  blocking collectives  66.2 us (24%)
  matrix products  41 us (15%)
  between operations  16.1 us (6%)
  starting transfers between devices  6.48 us (2%)
  local copies, waits for them, and re-layouts  2.9 us (1%)
    psum x1, waiting for transfers between devices, per_device(): rotated_acts = lax.psum(partial_acts, 'narrow')  87.8 us
    all_to_all x1, blocking collectives, summed_rows(): lax.all_to_all(nearer, far, split_axis=0, concat_axis=0, tiled=True)  54.5 us
    all_gather x1, waiting for transfers between devices, per_device(): gathered = lax.all_gather(activations, WIDE, axis=0, tiled=True)  52.6 us
    dot_general x1, matrix products, per_device(): jnp.dot(gathered, act_basis, precision=highest, preferred_element_type=jn...  21.9 us
    dot_general x4, matrix products, per_device(): jnp.dot(acts_window.T, grads_window, precision=highest, preferred_element...  15.1 us
    all_to_all x1, starting transfers between devices, from_everyone(): lax.all_to_all(jnp.broadcast_to(value[None], (devices, *value.shape)), ax...  6.44 us
    all_to_all x1, blocking collectives, from_everyone(): lax.all_to_all(jnp.broadcast_to(value[None], (devices, *value.shape)), ax...  5.84 us
    all_to_all x1, blocking collectives, sent_and_summed(): lax.all_to_all(blocks, axis, split_axis=0, concat_axis=0, tiled=True)  5.84 us
  transfers between devices with their start and end apart: 3, of which 2 were waited for; matrix products, arithmetic and copies ran while one was open for 11% of the time, Pallas kernels for 0%

commit v1 on v0

--- a/solution.py
+++ b/solution.py
@@ -78,7 +78,11 @@
     partial_acts = jnp.dot(
         gathered, act_basis, precision=highest, preferred_element_type=jnp.float32
     )
-    rotated_acts = lax.psum(partial_acts, "narrow")
+
+    def _treat_joints(field_in):
+        return lax.all_gather(field_in, "narrow").sum(axis=0)
+
+    rotated_acts = _treat_joints(partial_acts)
     partial_grads = jnp.dot(
         grads, grad_basis, precision=highest, preferred_element_type=jnp.float32
     )

time: 276 us -> 365 us (1.32)
  waiting for transfers between devices: 141 us -> 224 us
  local copies, waits for them, and re-layouts: 2.9 us -> 22.3 us
  blocking collectives: 66.2 us -> 51.3 us
  other arithmetic: 2.23 us -> 6.96 us
    all_gather x0 -> x1, waiting for transfers between devices: none -> 118 us  [_treat_joints(): return lax.all_gather(field_in, 'narrow').sum(axis=0)]
    psum x1 -> x0, waiting for transfers between devices: 87.8 us -> none  [per_device(): rotated_acts = lax.psum(partial_acts, 'narrow')]
    all_to_all x1, waiting for transfers between devices: 0.01 us -> 28.7 us  [from_everyone(): lax.all_to_all(jnp.broadcast_to(value[None], (devices, *value.shape)), ax...]
    all_gather x1, waiting for transfers between devices: 52.6 us -> 76.9 us  [per_device(): gathered = lax.all_gather(activations, WIDE, axis=0, tiled=True)]
    unnamed x6 -> x9, local copies, waits for them, and re-layouts: 1.03 us -> 20.4 us
    all_to_all x1, blocking collectives: 54.5 us -> 39.6 us  [summed_rows(): lax.all_to_all(nearer, far, split_axis=0, concat_axis=0, tiled=True)]
    reduce_sum x0 -> x1, other arithmetic: none -> 4.74 us  [_treat_joints(): return lax.all_gather(field_in, 'narrow').sum(axis=0)]
  transfers between devices with their start and end apart: 3 -> 3, of which waited for: 2 -> 3; matrix products, arithmetic and copies ran while one was open for 11% -> 2% of each run, Pallas kernels for 0% -> 0%
where the time goes in v1:
time: 365 us; the launch traced here: 363 us
  waiting for transfers between devices  224 us (61%)
  blocking collectives  51.3 us (14%)
  matrix products  38.5 us (11%)
  local copies, waits for them, and re-layouts  22.3 us (6%)
  between operations  15.9 us (4%)
  other arithmetic  6.96 us (2%)
  starting transfers between devices  4.44 us (1%)
    all_gather x1, waiting for transfers between devices, _treat_joints(): return lax.all_gather(field_in, 'narrow').sum(axis=0)  118 us
    all_gather x1, waiting for transfers between devices, per_device(): gathered = lax.all_gather(activations, WIDE, axis=0, tiled=True)  76.9 us
    all_to_all x1, blocking collectives, summed_rows(): lax.all_to_all(nearer, far, split_axis=0, concat_axis=0, tiled=True)  39.6 us
    all_to_all x1, waiting for transfers between devices, from_everyone(): lax.all_to_all(jnp.broadcast_to(value[None], (devices, *value.shape)), ax...  28.7 us
    dot_general x1, matrix products, per_device(): jnp.dot(gathered, act_basis, precision=highest, preferred_element_type=jn...  21.9 us
    unnamed x9, local copies, waits for them, and re-layouts  20.4 us
    dot_general x4, matrix products, per_device(): jnp.dot(acts_window.T, grads_window, precision=highest, preferred_element...  13.7 us
  transfers between devices with their start and end apart: 3, of which 3 were waited for; matrix products, arithmetic and copies ran while one was open for 2% of the time, Pallas kernels for 0%

profile of v1, /device:TPU:32, one launch (start us, length us, event | category | flops | bytes accessed | tf_op | source)
XLA Modules:
  0.0 363.4 jit_solution(13672851331560349913)
XLA Ops:
  6.5 0.0 copy-start
  6.5 0.0 all-gather.4.cloned.1.call-start
  6.5 0.7 all-gather.4.cloned.1.call-update
  7.3 0.0 all-gather.6.cloned.1.call-start
  7.3 76.9 %all-gather.4.cloned.1.call-done = f32[1024,2176]{1,0:T(8,128)} async-done(((f32[32,2176]{1,0:T(8,128)}), f32[1024,2176]{1,0:T(8,128)}) %all-gather.4.cloned.1.call-update) | async-done | bytes 8912912 | tf_op jit(solution)/shard_map/all_gather | solution.py:77
  84.2 21.9 %fusion.28 = f32[1024,544]{0,1:T(8,128)} fusion(f32[1024,2176]{1,0:T(8,128)} %all-gather.4.cloned.1.call-done, f32[2176,544]{0,1:T(8,128)} %param.6), kind=kOutput, calls=%fused_computation.42 | convolution fusion | flops 14545846272 | bytes 15876096 | tf_op jit(solution)/shard_map/dot_general | solution.py:78
  106.0 0.0 copy-start.2
  106.0 0.0 all-gather.6.cloned.1.call-update
  106.1 0.0 copy-done
  106.1 1.0 copy-done.2
  107.0 2.9 fusion.29
  110.0 0.2 copy.12
  110.2 5.8 %all_to_all.20 = f32[2,16,32,640]{3,2,1,0:T(8,128)S(1)} all-to-all(f32[2,16,32,640]{3,2,1,0:T(8,128)S(1)} %bitcast.21), channel_id=1, replica_groups=mesh['wide_0'=2,'wide_1'=8,'wide_2'=2,'narrow'=8] {'wide_2'}, dimensions={0} | all-to-all | bytes 5242880 | tf_op jit(solution)/shard_map/all_to_all | solution.py:45
  116.0 1.3 reduce_sum.65
  117.4 39.6 %all_to_all.21 = f32[16,32,640]{2,1,0:T(8,128)S(1)} all-to-all(f32[16,32,640]{2,1,0:T(8,128)} %reduce_sum.65), channel_id=1, replica_groups=mesh['wide_0'=2,'wide_1'=8,'wide_2'=2,'narrow'=8] {'wide_0','wide_1'}, dimensions={0} | all-to-all | bytes 2621440 | tf_op jit(solution)/shard_map/all_to_all | solution.py:53
  157.0 0.1 reduce_sum.66
  157.0 1.2 broadcast_in_dim.4
  158.2 0.0 copy-start.3
  158.2 4.4 %all-to-all-start.2 = ((f32[16,32,640]{2,1,0:T(8,128)}), f32[16,32,640]{2,1,0:T(8,128)S(1)}, u32[]{:S(2)}, u32[]{:S(2)}) async-start(f32[16,32,640]{2,1,0:T(8,128)} %broadcast_in_dim.4), calls=%async_computation.2 | async-start | bytes 2621440 | tf_op jit(solution)/shard_map/all_to_all | solution.py:19
  162.6 0.0 copy-done.3
  162.6 0.7 convert_reduce_fusion
  165.8 0.1 fusion.27
  165.8 28.7 %all-to-all-done.2 = f32[16,32,640]{2,1,0:T(8,128)S(1)} async-done(((f32[16,32,640]{2,1,0:T(8,128)}), f32[16,32,640]{2,1,0:T(8,128)S(1)}, u32[]{:S(2)}, u32[]{:S(2)}) %all-to-all-start.2) | async-done | bytes 1310752 | tf_op jit(solution)/shard_map/all_to_all | solution.py:19
  194.5 0.3 broadcast_in_dim.5
  194.8 5.8 %all_to_all.22 = f32[2,16,32,640]{3,2,1,0:T(8,128)S(1)} all-to-all(f32[2,16,32,640]{3,2,1,0:T(8,128)S(1)} %broadcast_in_dim.5), channel_id=1, replica_groups=mesh['wide_0'=2,'wide_1'=8,'wide_2'=2,'narrow'=8] {'wide_2'}, dimensions={0} | all-to-all | bytes 5242880 | tf_op jit(solution)/shard_map/all_to_all | solution.py:19
  200.7 0.2 copy.9
  200.9 117.8 %all-gather.6.cloned.1.call-done = f32[8192,544]{0,1:T(8,128)} async-done(((f32[1024,544]{0,1:T(8,128)}), f32[8192,544]{0,1:T(8,128)}) %all-gather.6.cloned.1.call-update) | async-done | bytes 17825808 | tf_op jit(solution)/shard_map/all_gather | solution.py:83
  318.6 19.4 %copy.10 = f32[68,8,8,1024]{3,2,1,0:T(8,128)S(1)} copy(f32[68,8,8,1024]{3,1,2,0:T(8,128)} %bitcast.20) | data formatting | bytes 35651584
  338.1 4.7 %bitcast_reduce_fusion = f32[1024,544]{0,1:T(8,128)S(1)} fusion(f32[68,8,8,1024]{3,2,1,0:T(8,128)S(1)} %copy.10), kind=kLoop, calls=%fused_computation | loop fusion | flops 3899392 | bytes 20054016 | tf_op jit(solution)/shard_map/reduce_sum | solution.py:83
  342.8 3.1 convolution_multiply_fusion.1
  345.9 3.1 convolution_multiply_fusion.2
  349.1 3.2 fusion.1
  352.3 0.0 copy-start.1
  352.3 4.2 %fusion.3 = f32[544,640]{1,0:T(8,128)} fusion(f32[544,640]{1,0:T(8,128)S(1)} %fusion.1, f32[1024,640]{1,0:T(8,128)S(1)} %bitcast.19, s32[]{:T(128)S(6)} %select_n.11, f32[1024,544]{0,1:T(8,128)S(1)} %bitcast_reduce_fusion, f32[512]{0:T(512)S(1)} %get-tuple-element.9), kind=kOutput, calls=%fused_computation.9 | convolution fusion | flops 2140467200 | bytes 5213184 | tf_op jit(solution)/shard_map/dot_general | solution.py:94
  356.6 0.0 copy-done.1
Async XLA Ops:
  6.5 99.5 %copy-start = (f32[1024,160]{0,1:T(8,128)S(1)}, f32[1024,160]{0,1:T(8,128)}, u32[]{:S(2)}) copy-start(f32[1024,160]{0,1:T(8,128)} %param.7) | copy-start | bytes 1966084
  6.5 77.6 %all-gather.4.cloned.1.call-start = ((), (), s32[]{:S(2)}) async-start(), calls=%async_computation.4 | async-start | bytes 9191424 | tf_op jit(solution)/shard_map/all_gather | solution.py:77
  7.3 311.4 %all-gather.6.cloned.1.call-start = ((), (), s32[]{:S(2)}) async-start(), calls=%async_computation.5 | async-start | bytes 20054016 | tf_op jit(solution)/shard_map/all_gather | solution.py:83
  106.0 1.0 copy-start.2
  158.2 4.4 %copy-start.3 = (s32[1024]{0:T(1024)S(1)}, s32[1024]{0:T(1024)}, u32[]{:S(2)}) copy-start(s32[1024]{0:T(1024)} %param.9) | copy-start | bytes 12292
  158.2 36.3 %all-to-all-start.2 = ((f32[16,32,640]{2,1,0:T(8,128)}), f32[16,32,640]{2,1,0:T(8,128)S(1)}, u32[]{:S(2)}, u32[]{:S(2)}) async-start(f32[16,32,640]{2,1,0:T(8,128)} %broadcast_in_dim.4), calls=%async_computation.2 | async-start | bytes 2621440 | tf_op jit(solution)/shard_map/all_to_all | solution.py:19
  352.3 4.3 %copy-start.1 = (f32[1024,160]{0,1:T(8,128)S(1)}, f32[1024,160]{0,1:T(8,128)}, u32[]{:S(2)}) copy-start(f32[1024,160]{0,1:T(8,128)} %param.7) | copy-start | bytes 1966084
Sparse Core Ops, SparseCore 0:
  9.2 74.9 all-gather.3
  106.2 212.3 all-gather.5
